TPU v7x, 512 devices: a whole 4x8x8 slice. The times are simulated.
512 devices in a mesh: section: 32 (over z, x), leaf: 16 (over y, core).
Axes of the slice: x: 4, y: 8, z: 8, core: 2. Of those that a mesh axis runs over, the one named last changes fastest.
Arguments:
- query_feats: bfloat16 [65536, 300], P(('section', 'leaf')), may hold values from -6 to 6
- query_weight: float32 [65536], P('section'), may hold values from 0.02 to 0.2
- positive_label: int32 [65536, 8], P('section'), may hold values from 0 to 131071, as said below
- positive_bucket: int32 [65536, 8], P('section'), may hold values from 0 to 15
- inv_prop: float32 [16], replicated, may hold values from 1 to 10
- primary_w: bfloat16 [131072, 300], P(('section', 'leaf')), may hold values from -0.375 to 0.375
- copy_owner: int32 [131072], P(('section', 'leaf')), may hold values from 0 to 31, as said below
- copy_row: int32 [131072], P(('section', 'leaf')), may hold values from 0 to 255
Outputs:
- query_grad: float32 [65536, 300], P(('section', 'leaf'))
- primary_grad: float32 [131072, 300], P(('section', 'leaf'))
Inputs may be any that keep to these rules, and one draw needn't show every extreme that they name: `copy_owner`: each copy names a section other than its own device's; among the copies of one device at most 16 name one owner, and exactly 16 name one of them. `positive_label`: every listed label is the label of some slot, primary or copy, of the query's own section; a label may be listed twice.
All inputs are finite; a program needn't handle non-finite values.
Results may differ from a plain program's by a relative error of at most 0.0018.
Values may be sent and summed in bfloat16 or wider, within the bound.
No kernel may reach another device: no remote copies, remote signals or barrier semaphores. Data moves between devices by JAX's collectives and lax.ppermute only.
A program may use at most 64 MiB of HBM per device.

v0:
```python
import math
import jax
import jax.numpy as jnp
from jax import lax
from jax.sharding import PartitionSpec as P


def on_device(
    query_feats,
    query_weight,
    positive_label,
    positive_bucket,
    inv_prop,
    primary_w,
    copy_owner,
    copy_row,
):
    sections = lax.axis_size("section")
    leaves = lax.axis_size("leaf")
    section_id = lax.axis_index("section")
    leaf_id = lax.axis_index("leaf")
    prim_rows = primary_w.shape[0]
    copy_count = copy_owner.shape[0]
    feature_dim = primary_w.shape[1]
    capacity = 8 * ((2 * copy_count // (sections - 1) + 7) // 8)
    owner_hot = (copy_owner[:, None] == jnp.arange(sections, dtype=jnp.int32)[None, :]).astype(
        jnp.float32
    )
    before = jnp.cumsum(owner_hot, axis=0) - owner_hot
    rank_in = jnp.sum(before * owner_hot, axis=1).astype(jnp.int32)
    target = copy_owner * capacity + rank_in
    requests = (
        jnp.zeros((sections * capacity,), jnp.int32)
        .at[target]
        .set(copy_row)
        .reshape(sections, capacity)
    )
    wanted = lax.all_to_all(requests, "section", split_axis=0, concat_axis=0, tiled=True)
    served = jnp.take(primary_w, wanted.reshape(-1), axis=0).reshape(
        sections, capacity, feature_dim
    )
    arrived = lax.all_to_all(served, "section", split_axis=0, concat_axis=0, tiled=True)
    copy_w = jnp.take(arrived.reshape(sections * capacity, feature_dim), target, axis=0)
    weights = jnp.concatenate([primary_w, copy_w], axis=0)
    first_label = (section_id * leaves + leaf_id) * prim_rows
    labels = jnp.concatenate(
        [
            first_label + jnp.arange(prim_rows, dtype=jnp.int32),
            (copy_owner * leaves + leaf_id) * prim_rows + copy_row,
        ]
    )
    bucket_hot = positive_bucket[..., None] == jnp.arange(inv_prop.shape[0], dtype=jnp.int32)
    pos_value = jnp.sum(jnp.where(bucket_hot, inv_prop, 0.0), axis=-1)
    slot_count = weights.shape[0]
    section_rows = positive_label.shape[0]
    start_state = (
        jnp.zeros((slot_count, feature_dim), jnp.float32),
        jnp.zeros((section_rows, feature_dim), jnp.float32),
    )
    shard_rows = lax.all_gather(query_feats, "leaf", axis=0, tiled=True)
    piece_rows = shard_rows.shape[0]
    block_rows = math.gcd(piece_rows, 256)

    def block_step(block_num, partial_sums):
        slot_acc, query_acc = partial_sums
        offset_row = block_num * block_rows
        q_block = lax.dynamic_slice_in_dim(shard_rows, offset_row, block_rows, 0)
        labels_block = lax.dynamic_slice_in_dim(positive_label, offset_row, block_rows, 0)
        values_block = lax.dynamic_slice_in_dim(pos_value, offset_row, block_rows, 0)
        scale_block = lax.dynamic_slice_in_dim(query_weight, offset_row, block_rows, 0)
        logits = lax.dot_general(
            q_block, weights, (((1,), (1,)), ((), ())), preferred_element_type=jnp.float32
        )
        sigmoid_val = jax.nn.sigmoid(logits)
        hit_count = jnp.zeros(logits.shape, jnp.float32)
        pos_weight = jnp.zeros(logits.shape, jnp.float32)
        for column in range(labels_block.shape[1]):
            matched = (labels[None, :] == labels_block[:, column : column + 1]).astype(jnp.float32)
            hit_count = hit_count + matched
            pos_weight = pos_weight + matched * values_block[:, column : column + 1]
        mixed = (1.0 - jnp.minimum(hit_count, 1.0)) * sigmoid_val + pos_weight * (sigmoid_val - 1.0)
        coefficient = (scale_block[:, None] * mixed).astype(jnp.bfloat16)
        query_part = jnp.dot(coefficient, weights, preferred_element_type=jnp.float32)
        query_acc = lax.dynamic_update_slice_in_dim(query_acc, query_part, offset_row, 0)
        slot_acc = slot_acc + lax.dot_general(
            coefficient, q_block, (((0,), (0,)), ((), ())), preferred_element_type=jnp.float32
        )
        return (slot_acc, query_acc)

    slot_grad, query_sum = lax.fori_loop(0, piece_rows // block_rows, block_step, start_state)
    send_back = (
        jnp.zeros((sections * capacity, feature_dim), jnp.float32)
        .at[target]
        .set(slot_grad[prim_rows:])
        .reshape(sections, capacity, feature_dim)
    )
    returned = lax.all_to_all(send_back, "section", split_axis=0, concat_axis=0, tiled=True)
    primary_grad = (
        slot_grad[:prim_rows].at[wanted.reshape(-1)].add(returned.reshape(-1, feature_dim))
    )
    query_whole = lax.psum(query_sum, "leaf")
    query_grad = lax.dynamic_slice_in_dim(
        query_whole, leaf_id * query_feats.shape[0], query_feats.shape[0], 0
    )
    return (query_grad, primary_grad)


def solution(mesh):
    placed = (
        P(("section", "leaf"), None),
        P("section"),
        P("section", None),
        P("section", None),
        P(),
        P(("section", "leaf"), None),
        P(("section", "leaf")),
        P(("section", "leaf")),
    )
    return jax.shard_map(
        on_device,
        mesh=mesh,
        in_specs=placed,
        out_specs=(P(("section", "leaf"), None), P(("section", "leaf"), None)),
        check_vma=False,
    )
```

profile of v0, /device:TPU:1, one launch (start us, length us, event | category | flops | bytes accessed | tf_op | source)
XLA Modules:
  0.0 241.0 jit_solution(1173304423045071907)
XLA Ops:
  7.2 1.6 copy.31
  11.8 1.6 scatter_custom_fusion
  14.0 13.7 %all-to-all-start = ((s32[32,1,16]{2,1,0:T(1,128)}), s32[32,1,16]{2,1,0:T(1,128)S(1)}, u32[]{:S(2)}, u32[]{:S(2)}) async-start(s32[32,1,16]{2,1,0:T(1,128)} %bitcast.2), calls=%async_computation | async-start | bytes 32768 | tf_op jit(solution)/shard_map/all_to_all | solution.py:38
  28.9 7.4 %all-to-all-done = s32[32,1,16]{2,1,0:T(1,128)S(1)} async-done(((s32[32,1,16]{2,1,0:T(1,128)}), s32[32,1,16]{2,1,0:T(1,128)S(1)}, u32[]{:S(2)}, u32[]{:S(2)}) %all-to-all-start) | async-done | bytes 2080 | tf_op jit(solution)/shard_map/all_to_all | solution.py:38
  37.6 1.9 gather_fusion
  40.5 3.9 %all-to-all-start.1 = ((bf16[32,16,300]{2,1,0:T(8,128)(2,1)}), bf16[32,16,300]{2,1,0:T(8,128)(2,1)S(1)}, u32[]{:S(2)}, u32[]{:S(2)}) async-start(bf16[32,16,300]{2,1,0:T(8,128)(2,1)} %broadcast_select_fusion), calls=%async_computation.1 | async-start | bytes 786432 | tf_op jit(solution)/shard_map/all_to_all | solution.py:42
  45.4 10.8 %all-to-all-done.1 = bf16[32,16,300]{2,1,0:T(8,128)(2,1)S(1)} async-done(((bf16[32,16,300]{2,1,0:T(8,128)(2,1)}), bf16[32,16,300]{2,1,0:T(8,128)(2,1)S(1)}, u32[]{:S(2)}, u32[]{:S(2)}) %all-to-all-start.1) | async-done | bytes 307232 | tf_op jit(solution)/shard_map/all_to_all | solution.py:42
  56.3 1.2 gather_fusion.1
  58.3 51.9 %while.18 = (s32[]{:T(128)}, f32[512,300]{0,1:T(8,128)S(1)}, f32[2048,300]{0,1:T(8,128)S(1)}, f32[2048]{0:T(1024)}, s32[512]{0:T(512)S(1)}, /*index=5*/s32[2048,...) while((s32[]{:T(128)}, f32[512,300]{0,1:T(8,128)S(1)}, ...), condition=%wide.region_6.7_spmd.clone, body=%wide.region_5.6_spmd.clone.sunk | while | flops 242659344 | bytes 3474841 | solution.py:90
  61.3 2.0 fusion.53
  63.2 1.2 convolution_add_fusion.2
  67.8 2.0 fusion.53
  69.7 1.2 convolution_add_fusion.2
  74.2 2.0 fusion.53
  76.2 1.2 convolution_add_fusion.2
  80.7 2.0 fusion.53
  82.7 1.2 convolution_add_fusion.2
  87.2 2.0 fusion.53
  89.2 1.2 convolution_add_fusion.2
  93.7 2.0 fusion.53
  95.7 1.2 convolution_add_fusion.2
  100.2 2.0 fusion.53
  102.1 1.2 convolution_add_fusion.2
  106.7 2.0 fusion.53
  108.6 1.2 convolution_add_fusion.2
  110.2 1.4 copy-done
  111.9 2.3 scatter_custom_fusion.1
  114.2 10.0 %all-to-all-start.2 = ((f32[32,16,300]{2,1,0:T(8,128)}), f32[32,16,300]{2,1,0:T(8,128)S(1)}, u32[]{:S(2)}, u32[]{:S(2)}) async-start(f32[32,16,300]{2,1,0:T(8,128)} %bitcast.7), calls=%async_computation.2 | async-start | bytes 1572864 | tf_op jit(solution)/shard_map/all_to_all | solution.py:97
  124.5 21.2 %all-to-all-done.2 = f32[32,16,300]{2,1,0:T(8,128)S(1)} async-done(((f32[32,16,300]{2,1,0:T(8,128)}), f32[32,16,300]{2,1,0:T(8,128)S(1)}, u32[]{:S(2)}, u32[]{:S(2)}) %all-to-all-start.2) | async-done | bytes 614432 | tf_op jit(solution)/shard_map/all_to_all | solution.py:97
  145.7 3.8 %scatter_fusion = f32[256,300]{1,0:T(8,128)S(1)} fusion(f32[256,300]{1,0:T(8,128)S(1)} %slice.197, s32[512]{0:T(512)S(1)} %bitcast.110, f32[512,300]{1,0:T(8,128)S(1)} %bitcast.90), kind=kCustom, calls=%fused_computation.4 | custom fusion | flops 153600 | bytes 1845248 | tf_op jit(solution)/shard_map/scatter-add | solution.py:99
  150.3 82.2 %all-reduce.2.cloned.1.call-done = f32[2048,300]{0,1:T(8,128)} async-done(((f32[2048,300]{0,1:T(8,128)}), f32[2048,300]{0,1:T(8,128)}) %all-reduce.2.cloned.1.call-update) | async-done | bytes 2457616 | tf_op jit(solution)/shard_map/psum | solution.py:101
  232.5 1.6 constant_dynamic-slice_fusion.2
  (76 shorter events, 35.9 us)
Async XLA Ops:
  7.2 50.9 %all-gather.2.cloned.1.call-start = ((), (), s32[]{:S(2)}) async-start(), calls=%async_computation.3 | async-start | bytes 1671168 | tf_op jit(solution)/shard_map/all_gather | solution.py:60
  14.0 22.2 %all-to-all-start = ((s32[32,1,16]{2,1,0:T(1,128)}), s32[32,1,16]{2,1,0:T(1,128)S(1)}, u32[]{:S(2)}, u32[]{:S(2)}) async-start(s32[32,1,16]{2,1,0:T(1,128)} %bitcast.2), calls=%async_computation | async-start | bytes 32768 | tf_op jit(solution)/shard_map/all_to_all | solution.py:38
  37.6 6.9 %copy-start.2 = (s32[256]{0:T(256)S(1)}, s32[256]{0:T(256)}, u32[]{:S(2)}) copy-start(s32[256]{0:T(256)} %param.16) | copy-start | bytes 3076
  37.6 6.9 %copy-start.3 = (s32[256]{0:T(256)S(1)}, s32[256]{0:T(256)}, u32[]{:S(2)}) copy-start(s32[256]{0:T(256)} %param.17) | copy-start | bytes 3076
  37.6 6.9 %copy-start.1 = (s32[2048,8]{0,1:T(8,128)S(1)}, s32[2048,8]{0,1:T(8,128)}, u32[]{:S(2)}) copy-start(s32[2048,8]{0,1:T(8,128)} %param.13) | copy-start | bytes 196612
  37.6 6.9 %copy-start.4 = (f32[16]{0:T(128)S(1)}, f32[16]{0:T(128)}, u32[]{:S(2)}) copy-start(f32[16]{0:T(128)} %param.14) | copy-start | bytes 196
  40.5 15.8 %all-to-all-start.1 = ((bf16[32,16,300]{2,1,0:T(8,128)(2,1)}), bf16[32,16,300]{2,1,0:T(8,128)(2,1)S(1)}, u32[]{:S(2)}, u32[]{:S(2)}) async-start(bf16[32,16,300]{2,1,0:T(8,128)(2,1)} %broadcast_select_fusion), calls=%async_computation.1 | async-start | bytes 786432 | tf_op jit(solution)/shard_map/all_to_all | solution.py:42
  44.4 188.2 %all-reduce.2.cloned.1.call-start = ((), (), s32[]{:S(2)}) async-start(), calls=%async_computation.4 | async-start | bytes 4980736 | tf_op jit(solution)/shard_map/psum | solution.py:101
  110.2 1.5 copy-start
  114.2 31.5 %all-to-all-start.2 = ((f32[32,16,300]{2,1,0:T(8,128)}), f32[32,16,300]{2,1,0:T(8,128)S(1)}, u32[]{:S(2)}, u32[]{:S(2)}) async-start(f32[32,16,300]{2,1,0:T(8,128)} %bitcast.7), calls=%async_computation.2 | async-start | bytes 1572864 | tf_op jit(solution)/shard_map/all_to_all | solution.py:97
Sparse Core Ops, SparseCore 0:
  10.7 47.2 all-gather.1
  111.8 120.6 all-reduce.1
where the time goes:
time: 243 us; the launch traced here: 241 us
  waiting for transfers between devices  122 us (50%)
  local copies, waits for them, and re-layouts  39.2 us (16%)
  matrix products  28 us (12%)
  starting transfers between devices  27.7 us (11%)
  between operations  14.3 us (6%)
  other arithmetic  9.21 us (4%)
    psum x1, waiting for transfers between devices, on_device(): query_whole = lax.psum(query_sum, 'leaf')  82.2 us
    all_to_all x1, waiting for transfers between devices, on_device(): lax.all_to_all(send_back, 'section', split_axis=0, concat_axis=0, tiled=T...  21.2 us
    dot_general x8, matrix products, block_step(): lax.dot_general(q_block, weights, (((1,), (1,)), ((), ())), preferred_ele...  15.7 us
    all_to_all x1, starting transfers between devices, on_device(): lax.all_to_all(requests, 'section', split_axis=0, concat_axis=0, tiled=True)  13.7 us
    all_to_all x1, waiting for transfers between devices, on_device(): lax.all_to_all(served, 'section', split_axis=0, concat_axis=0, tiled=True)  10.8 us
    all_to_all x1, starting transfers between devices, on_device(): lax.all_to_all(send_back, 'section', split_axis=0, concat_axis=0, tiled=T...  10 us
    dot_general x8, matrix products, block_step(): lax.dot_general(coefficient, q_block, (((0,), (0,)), ((), ())), preferred...  10 us
    slice x8, local copies, waits for them, and re-layouts, block_step(): labels_block[:, column:column + 1]  8.72 us
  transfers between devices with their start and end apart: 5, of which 5 were waited for; matrix products, arithmetic and copies ran while one was open for 8% of the time, Pallas kernels for 0%

commit v1 on v0

--- a/solution.py
+++ b/solution.py
@@ -98,7 +98,11 @@
     primary_grad = (
         slot_grad[:prim_rows].at[wanted.reshape(-1)].add(returned.reshape(-1, feature_dim))
     )
-    query_whole = lax.psum(query_sum, "leaf")
+    query_whole = query_sum
+    for hop in (1, 2, 4, 8):
+        query_whole = query_whole + lax.ppermute(
+            query_whole, "leaf", [(dev, dev ^ hop) for dev in range(16)]
+        )
     query_grad = lax.dynamic_slice_in_dim(
         query_whole, leaf_id * query_feats.shape[0], query_feats.shape[0], 0
     )

time: 243 us -> 419 us (1.72)
  waiting for transfers between devices: 122 us -> 280 us
  starting transfers between devices: 27.7 us -> 43.6 us
  other arithmetic: 9.21 us -> 13.6 us
    ppermute x0 -> x4, waiting for transfers between devices: none -> 241 us  [on_device(): lax.ppermute(query_whole, 'leaf', [(dev, dev ^ hop) for dev in range(16)])]
    psum x1 -> x0, waiting for transfers between devices: 82.2 us -> none  [on_device(): query_whole = lax.psum(query_sum, 'leaf')]
    ppermute x0 -> x4, starting transfers between devices: none -> 22.1 us  [on_device(): lax.ppermute(query_whole, 'leaf', [(dev, dev ^ hop) for dev in range(16)])]
    all_to_all x1, starting transfers between devices: 10 us -> 3.91 us  [on_device(): lax.all_to_all(send_back, 'section', split_axis=0, concat_axis=0, tiled=T...]
    add x0 -> x4, other arithmetic: none -> 4.35 us  [on_device(): query_whole + lax.ppermute(query_whole, 'leaf', [(dev, dev ^ hop) for dev...]
  transfers between devices with their start and end apart: 5 -> 8, of which waited for: 5 -> 8; matrix products, arithmetic and copies ran while one was open for 8% -> 5% of each run, Pallas kernels for 0% -> 0%
where the time goes in v1:
time: 419 us; the launch traced here: 417 us
  waiting for transfers between devices  280 us (67%)
  starting transfers between devices  43.6 us (10%)
  local copies, waits for them, and re-layouts  36.2 us (9%)
  matrix products  28 us (7%)
  between operations  14.3 us (3%)
  other arithmetic  13.6 us (3%)
    ppermute x4, waiting for transfers between devices, on_device(): lax.ppermute(query_whole, 'leaf', [(dev, dev ^ hop) for dev in range(16)])  241 us
    ppermute x4, starting transfers between devices, on_device(): lax.ppermute(query_whole, 'leaf', [(dev, dev ^ hop) for dev in range(16)])  22.1 us
    all_to_all x1, waiting for transfers between devices, on_device(): lax.all_to_all(send_back, 'section', split_axis=0, concat_axis=0, tiled=T...  20.8 us
    dot_general x8, matrix products, block_step(): lax.dot_general(q_block, weights, (((1,), (1,)), ((), ())), preferred_ele...  15.7 us
    all_to_all x1, starting transfers between devices, on_device(): lax.all_to_all(requests, 'section', split_axis=0, concat_axis=0, tiled=True)  13.7 us
    all_to_all x1, waiting for transfers between devices, on_device(): lax.all_to_all(served, 'section', split_axis=0, concat_axis=0, tiled=True)  10.9 us
    dot_general x8, matrix products, block_step(): lax.dot_general(coefficient, q_block, (((0,), (0,)), ((), ())), preferred...  10 us
    slice x8, local copies, waits for them, and re-layouts, block_step(): labels_block[:, column:column + 1]  8.72 us
  transfers between devices with their start and end apart: 8, of which 8 were waited for; matrix products, arithmetic and copies ran while one was open for 5% of the time, Pallas kernels for 0%

profile of v1, /device:TPU:1, one launch (start us, length us, event | category | flops | bytes accessed | tf_op | source)
XLA Modules:
  0.0 416.6 jit_solution(17166405411111590949)
XLA Ops:
  7.2 1.6 copy.31
  11.8 1.6 scatter_custom_fusion
  14.0 13.7 %all-to-all-start = ((s32[32,1,16]{2,1,0:T(1,128)}), s32[32,1,16]{2,1,0:T(1,128)S(1)}, u32[]{:S(2)}, u32[]{:S(2)}) async-start(s32[32,1,16]{2,1,0:T(1,128)} %bitcast.2), calls=%async_computation | async-start | bytes 32768 | tf_op jit(solution)/shard_map/all_to_all | solution.py:38
  28.9 7.4 %all-to-all-done = s32[32,1,16]{2,1,0:T(1,128)S(1)} async-done(((s32[32,1,16]{2,1,0:T(1,128)}), s32[32,1,16]{2,1,0:T(1,128)S(1)}, u32[]{:S(2)}, u32[]{:S(2)}) %all-to-all-start) | async-done | bytes 2080 | tf_op jit(solution)/shard_map/all_to_all | solution.py:38
  37.6 1.9 gather_fusion
  40.5 3.9 all-to-all-start.1
  45.4 10.9 %all-to-all-done.1 = bf16[32,16,300]{2,1,0:T(8,128)(2,1)S(1)} async-done(((bf16[32,16,300]{2,1,0:T(8,128)(2,1)}), bf16[32,16,300]{2,1,0:T(8,128)(2,1)S(1)}, u32[]{:S(2)}, u32[]{:S(2)}) %all-to-all-start.1) | async-done | bytes 307232 | tf_op jit(solution)/shard_map/all_to_all | solution.py:42
  58.3 51.9 %while.18 = (s32[]{:T(128)}, f32[512,300]{0,1:T(8,128)S(1)}, f32[2048,300]{0,1:T(8,128)S(1)}, f32[2048]{0:T(1024)}, s32[512]{0:T(512)S(1)}, /*index=5*/s32[2048,...) while((s32[]{:T(128)}, f32[512,300]{0,1:T(8,128)S(1)}, ...), condition=%wide.region_6.7_spmd.clone, body=%wide.region_5.6_spmd.clone.sunk | while | flops 242659344 | bytes 3474841 | solution.py:90
  61.3 2.0 fusion.53
  63.2 1.2 convolution_add_fusion.2
  67.8 2.0 fusion.53
  69.7 1.2 convolution_add_fusion.2
  74.2 2.0 fusion.53
  80.7 2.0 fusion.53
  87.2 2.0 fusion.53
  93.7 2.0 fusion.53
  100.2 2.0 fusion.53
  106.7 2.0 fusion.53
  110.2 6.3 %collective-permute-start = (f32[2048,300]{0,1:T(8,128)S(1)}, f32[2048,300]{0,1:T(8,128)S(1)}, u32[]{:S(2)}, u32[]{:S(2)}) collective-permute-start(f32[2048,300]{0,1:T(8,128)S(1)} %get-tuple-element.223), channel_id=1, source_target_pairs={{0,1},{1,0},{2,3},{3,2},{4,5},{5,4},{6,7},{7,6},{8,9},{9,8},{10,11... | collective-permute-start | bytes 7372808 | tf_op jit(solution)/shard_map/ppermute | solution.py:103
  116.5 4.3 %collective-permute-done = f32[2048,300]{0,1:T(8,128)S(1)} collective-permute-done((f32[2048,300]{0,1:T(8,128)S(1)}, f32[2048,300]{0,1:T(8,128)S(1)}, u32[]{:S(2)}, u32[]{:S(2)}) %collective-permute-start) | collective-permute-done | bytes 2457632 | tf_op jit(solution)/shard_map/ppermute | solution.py:103
  121.2 3.2 collective-permute-start.1
  124.4 54.0 %collective-permute-done.1 = f32[2048,300]{0,1:T(8,128)S(1)} collective-permute-done((f32[2048,300]{0,1:T(8,128)S(1)}, f32[2048,300]{0,1:T(8,128)S(1)}, u32[]{:S(2)}, u32[]{:S(2)}) %collective-permute-start.1) | collective-permute-done | bytes 2457632 | tf_op jit(solution)/shard_map/ppermute | solution.py:103
  178.8 4.2 %collective-permute-start.2 = (f32[2048,300]{0,1:T(8,128)S(1)}, f32[2048,300]{0,1:T(8,128)S(1)}, u32[]{:S(2)}, u32[]{:S(2)}) collective-permute-start(f32[2048,300]{0,1:T(8,128)S(1)} %add.296), channel_id=1, source_target_pairs={{0,4},{1,5},{2,6},{3,7},{4,0},{5,1},{6,2},{7,3},{8,12},{9,13},{10,... | collective-permute-start | bytes 7372808 | tf_op jit(solution)/shard_map/ppermute | solution.py:103
  183.0 106.8 %collective-permute-done.2 = f32[2048,300]{0,1:T(8,128)S(1)} collective-permute-done((f32[2048,300]{0,1:T(8,128)S(1)}, f32[2048,300]{0,1:T(8,128)S(1)}, u32[]{:S(2)}, u32[]{:S(2)}) %collective-permute-start.2) | collective-permute-done | bytes 2457632 | tf_op jit(solution)/shard_map/ppermute | solution.py:103
  289.9 1.8 add.297
  291.7 8.4 %collective-permute-start.3 = (f32[2048,300]{0,1:T(8,128)}, f32[2048,300]{0,1:T(8,128)}, u32[]{:S(2)}, u32[]{:S(2)}) collective-permute-start(f32[2048,300]{0,1:T(8,128)} %add.297), channel_id=1, source_target_pairs={{0,8},{1,9},{2,10},{3,11},{4,12},{5,13},{6,14},{7,15},{8,0},{9,1},... | collective-permute-start | bytes 7372808 | tf_op jit(solution)/shard_map/ppermute | solution.py:103
  300.3 2.3 scatter_custom_fusion.1
  302.6 3.9 all-to-all-start.2
  306.9 20.8 %all-to-all-done.2 = f32[32,16,300]{2,1,0:T(8,128)S(1)} async-done(((f32[32,16,300]{2,1,0:T(8,128)}), f32[32,16,300]{2,1,0:T(8,128)S(1)}, u32[]{:S(2)}, u32[]{:S(2)}) %all-to-all-start.2) | async-done | bytes 614432 | tf_op jit(solution)/shard_map/all_to_all | solution.py:97
  327.6 3.8 scatter_fusion
  332.3 75.8 %collective-permute-done.3 = f32[2048,300]{0,1:T(8,128)} collective-permute-done((f32[2048,300]{0,1:T(8,128)}, f32[2048,300]{0,1:T(8,128)}, u32[]{:S(2)}, u32[]{:S(2)}) %collective-permute-start.3) | collective-permute-done | bytes 2457632 | tf_op jit(solution)/shard_map/ppermute | solution.py:103
  408.1 1.7 dynamic-slice_add_fusion
  (82 shorter events, 45.3 us)
Async XLA Ops:
  7.2 50.9 %all-gather.2.cloned.1.call-start = ((), (), s32[]{:S(2)}) async-start(), calls=%async_computation.3 | async-start | bytes 1671168 | tf_op jit(solution)/shard_map/all_gather | solution.py:60
  14.0 22.2 %all-to-all-start = ((s32[32,1,16]{2,1,0:T(1,128)}), s32[32,1,16]{2,1,0:T(1,128)S(1)}, u32[]{:S(2)}, u32[]{:S(2)}) async-start(s32[32,1,16]{2,1,0:T(1,128)} %bitcast.2), calls=%async_computation | async-start | bytes 32768 | tf_op jit(solution)/shard_map/all_to_all | solution.py:38
  37.6 6.8 %copy-start.1 = (s32[256]{0:T(256)S(1)}, s32[256]{0:T(256)}, u32[]{:S(2)}) copy-start(s32[256]{0:T(256)} %param.16) | copy-start | bytes 3076
  37.6 6.8 %copy-start.2 = (s32[256]{0:T(256)S(1)}, s32[256]{0:T(256)}, u32[]{:S(2)}) copy-start(s32[256]{0:T(256)} %param.17) | copy-start | bytes 3076
  37.6 6.8 %copy-start = (s32[2048,8]{0,1:T(8,128)S(1)}, s32[2048,8]{0,1:T(8,128)}, u32[]{:S(2)}) copy-start(s32[2048,8]{0,1:T(8,128)} %param.13) | copy-start | bytes 196612
  37.6 6.8 %copy-start.3 = (f32[16]{0:T(128)S(1)}, f32[16]{0:T(128)}, u32[]{:S(2)}) copy-start(f32[16]{0:T(128)} %param.14) | copy-start | bytes 196
  40.5 15.8 %all-to-all-start.1 = ((bf16[32,16,300]{2,1,0:T(8,128)(2,1)}), bf16[32,16,300]{2,1,0:T(8,128)(2,1)S(1)}, u32[]{:S(2)}, u32[]{:S(2)}) async-start(bf16[32,16,300]{2,1,0:T(8,128)(2,1)} %broadcast_select_fusion), calls=%async_computation.1 | async-start | bytes 786432 | tf_op jit(solution)/shard_map/all_to_all | solution.py:42
  110.2 10.6 %collective-permute-start = (f32[2048,300]{0,1:T(8,128)S(1)}, f32[2048,300]{0,1:T(8,128)S(1)}, u32[]{:S(2)}, u32[]{:S(2)}) collective-permute-start(f32[2048,300]{0,1:T(8,128)S(1)} %get-tuple-element.223), channel_id=1, source_target_pairs={{0,1},{1,0},{2,3},{3,2},{4,5},{5,4},{6,7},{7,6},{8,9},{9,8},{10,11... | collective-permute-start | bytes 7372808 | tf_op jit(solution)/shard_map/ppermute | solution.py:103
  121.2 57.2 %collective-permute-start.1 = (f32[2048,300]{0,1:T(8,128)S(1)}, f32[2048,300]{0,1:T(8,128)S(1)}, u32[]{:S(2)}, u32[]{:S(2)}) collective-permute-start(f32[2048,300]{0,1:T(8,128)S(1)} %add.295), channel_id=1, source_target_pairs={{0,2},{1,3},{2,0},{3,1},{4,6},{5,7},{6,4},{7,5},{8,10},{9,11},{10,... | collective-permute-start | bytes 7372808 | tf_op jit(solution)/shard_map/ppermute | solution.py:103
  178.8 111.1 %collective-permute-start.2 = (f32[2048,300]{0,1:T(8,128)S(1)}, f32[2048,300]{0,1:T(8,128)S(1)}, u32[]{:S(2)}, u32[]{:S(2)}) collective-permute-start(f32[2048,300]{0,1:T(8,128)S(1)} %add.296), channel_id=1, source_target_pairs={{0,4},{1,5},{2,6},{3,7},{4,0},{5,1},{6,2},{7,3},{8,12},{9,13},{10,... | collective-permute-start | bytes 7372808 | tf_op jit(solution)/shard_map/ppermute | solution.py:103
  291.7 116.4 %collective-permute-start.3 = (f32[2048,300]{0,1:T(8,128)}, f32[2048,300]{0,1:T(8,128)}, u32[]{:S(2)}, u32[]{:S(2)}) collective-permute-start(f32[2048,300]{0,1:T(8,128)} %add.297), channel_id=1, source_target_pairs={{0,8},{1,9},{2,10},{3,11},{4,12},{5,13},{6,14},{7,15},{8,0},{9,1},... | collective-permute-start | bytes 7372808 | tf_op jit(solution)/shard_map/ppermute | solution.py:103
  302.6 25.0 %all-to-all-start.2 = ((f32[32,16,300]{2,1,0:T(8,128)}), f32[32,16,300]{2,1,0:T(8,128)S(1)}, u32[]{:S(2)}, u32[]{:S(2)}) async-start(f32[32,16,300]{2,1,0:T(8,128)} %bitcast.7), calls=%async_computation.2 | async-start | bytes 1572864 | tf_op jit(solution)/shard_map/all_to_all | solution.py:97
Sparse Core Ops, SparseCore 0:
  10.7 47.2 all-gather.1
